TPU v7x, 256 devices: a whole 4x4x8 slice. The times are simulated.
256 devices in a mesh: resp: 16 (over y, z_hi), ctx: 16 (over x, z_lo, core).
Axes of the slice: x: 4, y: 4, z: 8 (z_hi: 4, z_lo: 2; z = z_hi * 2 + z_lo), core: 2. Of those that a mesh axis runs over, the one named last changes fastest.
Arguments:
- queries: bfloat16 [16, 2048, 2560], P('resp', 'ctx'), may hold values from -96 to 96
- resp_keys: bfloat16 [16, 2048, 512], P('resp', 'ctx'), may hold values from -6 to 6
- resp_values: bfloat16 [16, 2048, 512], P('resp', 'ctx'), may hold values from -6 to 6
- prompt_keys: bfloat16 [512, 512], P('ctx'), may hold values from -6 to 6
- prompt_values: bfloat16 [512, 512], P('ctx'), may hold values from -6 to 6
- out_grad: bfloat16 [16, 2048, 2560], P('resp', 'ctx'), may hold values from -24 to 24
- lengths: int32 [16], P('resp'), may hold values from 256 to 2048, as said below
Outputs:
- attn_out: bfloat16 [16, 2048, 2560], P('resp', 'ctx')
- query_grad: bfloat16 [16, 2048, 2560], P('resp', 'ctx')
- resp_key_grad: bfloat16 [16, 2048, 512], P('resp', 'ctx')
- resp_value_grad: bfloat16 [16, 2048, 512], P('resp', 'ctx')
- prompt_key_grad: bfloat16 [512, 512], P('ctx')
- prompt_value_grad: bfloat16 [512, 512], P('ctx')
Inputs may be any that keep to these rules, and one draw needn't show every extreme that they name: `lengths`: some response has all 2048 tokens.
All inputs are finite; a program needn't handle non-finite values.
Results may differ from a plain program's by a relative error of at most 0.023.
Values may be sent and summed in bfloat16 or wider, within the bound.
A program may use at most 128 MiB of HBM per device.

v0:
```python
import math
import jax
import jax.numpy as jnp
from jax import lax
from jax.sharding import PartitionSpec as P

DH = 128
HQ = 20
HK = 4
NEG = -1e30


def score_block(query4, keys_blk, key_pos, row_pos, scale):
    keys3 = keys_blk.reshape(keys_blk.shape[0], query4.shape[1], query4.shape[3])
    raw = jnp.einsum("nkgd,mkd->kgnm", query4, keys3, preferred_element_type=jnp.float32) * scale
    allowed = key_pos[None, :] <= row_pos[:, None]
    return jnp.where(allowed[None, None], raw, jnp.float32(NEG))


def scan_blocks(keys_all, values_all, pos_all, step, init):
    total_rows = keys_all.shape[0]
    block = math.gcd(total_rows, 512)
    count = total_rows // block
    blocks = (
        keys_all.reshape(count, block, keys_all.shape[1]),
        values_all.reshape(count, block, values_all.shape[1]),
        pos_all.reshape(count, block),
    )
    return lax.scan(step, init, blocks)


def body(queries, resp_keys, resp_values, prompt_keys, prompt_values, out_grad, lengths):
    rows = queries.shape[1]
    group = HQ // HK
    width = HK * DH
    scale = DH ** (-0.5)
    cycle = lax.axis_size("ctx")
    first_row = lax.axis_index("ctx") * rows
    row_pos = first_row + jnp.arange(rows, dtype=jnp.int32)
    row_ok = row_pos < lengths[0]
    query4 = queries[0].reshape(rows, HK, group, DH)
    grad = jnp.where(row_ok[:, None], out_grad[0], jnp.zeros_like(out_grad[0]))
    grad4 = grad.reshape(rows, HK, group, DH)
    seq_rows = resp_keys.shape[1] * cycle
    prompt_rows = prompt_keys.shape[0] * cycle

    def stats_update(stats, keys_blk, key_pos):
        top, total = stats
        scores = score_block(query4, keys_blk, key_pos, row_pos, scale)
        new_top = jnp.maximum(top, jnp.max(scores, axis=-1))
        total = total * jnp.exp(top - new_top) + jnp.sum(
            jnp.exp(scores - new_top[..., None]), axis=-1
        )
        return (new_top, total)

    top0 = jnp.full((HK, group, rows), NEG, jnp.float32)
    total0 = jnp.zeros((HK, group, rows), jnp.float32)
    pieces = (
        lax.all_gather(prompt_keys, "ctx", axis=0, tiled=True),
        lax.all_gather(prompt_values, "ctx", axis=0, tiled=True),
    )
    top = top0
    total = total0
    key_pos = jnp.full((pieces[0].shape[0],), -1, jnp.int32)
    top, total = stats_update((top, total), pieces[0], key_pos)
    key_buf = pieces[0]
    value_buf = pieces[1]
    top, total, prompt_kbuf, prompt_vbuf = (top, total, key_buf, value_buf)
    pieces = (
        lax.all_gather(resp_keys[0], "ctx", axis=0, tiled=True),
        lax.all_gather(resp_values[0], "ctx", axis=0, tiled=True),
    )
    top, total, key_buf, value_buf = (
        top,
        total,
        jnp.zeros((seq_rows, width), jnp.bfloat16),
        jnp.zeros((seq_rows, width), jnp.bfloat16),
    )
    key_pos = jnp.arange(pieces[0].shape[0], dtype=jnp.int32)
    top, total = stats_update((top, total), pieces[0], key_pos)
    key_buf = pieces[0]
    value_buf = pieces[1]
    top, total, resp_kbuf, resp_vbuf = (top, total, key_buf, value_buf)
    lse = top + jnp.log(total)
    prompt_pos = jnp.full((prompt_rows,), -1, jnp.int32)
    resp_pos = jnp.arange(seq_rows, dtype=jnp.int32)

    def out_step(acc, blk):
        keys_blk, values_blk, key_pos = blk
        scores = score_block(query4, keys_blk, key_pos, row_pos, scale)
        prob = jnp.exp(scores - lse[..., None]).astype(jnp.bfloat16)
        values3 = values_blk.reshape(values_blk.shape[0], HK, DH)
        return (
            acc + jnp.einsum("kgnm,mkd->nkgd", prob, values3, preferred_element_type=jnp.float32),
            None,
        )

    mixed0 = jnp.zeros((rows, HK, group, DH), jnp.float32)
    mixed, unused = scan_blocks(prompt_kbuf, prompt_vbuf, prompt_pos, out_step, mixed0)
    mixed, unused = scan_blocks(resp_kbuf, resp_vbuf, resp_pos, out_step, mixed)
    attn_out = jnp.where(row_ok[:, None], mixed.reshape(rows, HQ * DH), jnp.float32(0.0)).astype(
        jnp.bfloat16
    )
    delta = jnp.einsum(
        "nkgd,nkgd->kgn",
        grad4,
        attn_out.reshape(rows, HK, group, DH),
        preferred_element_type=jnp.float32,
    )

    def grads_block(keys_blk, values_blk, key_pos):
        scores = score_block(query4, keys_blk, key_pos, row_pos, scale)
        prob = jnp.exp(scores - lse[..., None])
        prob_low = prob.astype(jnp.bfloat16)
        keys3 = keys_blk.reshape(keys_blk.shape[0], HK, DH)
        values3 = values_blk.reshape(values_blk.shape[0], HK, DH)
        dprob = jnp.einsum("nkgd,mkd->kgnm", grad4, values3, preferred_element_type=jnp.float32)
        dscore = (prob * (dprob - delta[..., None])).astype(jnp.bfloat16)
        dquery = (
            jnp.einsum("kgnm,mkd->nkgd", dscore, keys3, preferred_element_type=jnp.float32) * scale
        )
        dkey = (
            jnp.einsum("kgnm,nkgd->mkd", dscore, query4, preferred_element_type=jnp.float32) * scale
        )
        dvalue = jnp.einsum("kgnm,nkgd->mkd", prob_low, grad4, preferred_element_type=jnp.float32)
        both = jnp.concatenate(
            [dkey.reshape(keys_blk.shape[0], width), dvalue.reshape(keys_blk.shape[0], width)],
            axis=1,
        )
        return (dquery, both)

    def back_step(acc, blk):
        keys_blk, values_blk, key_pos = blk
        dquery, both = grads_block(keys_blk, values_blk, key_pos)
        return (acc + dquery, both)

    dquery0 = jnp.zeros((rows, HK, group, DH), jnp.float32)
    dquery, prompt_terms = scan_blocks(prompt_kbuf, prompt_vbuf, prompt_pos, back_step, dquery0)
    prompt_term = prompt_terms.reshape(prompt_rows, 2 * width)
    dquery, resp_terms = scan_blocks(resp_kbuf, resp_vbuf, resp_pos, back_step, dquery)
    resp_sum = lax.psum_scatter(
        resp_terms.reshape(seq_rows, 2 * width), "ctx", scatter_dimension=0, tiled=True
    )
    query_grad = dquery.reshape(rows, HQ * DH).astype(jnp.bfloat16)
    prompt_part = lax.psum_scatter(prompt_term, "ctx", scatter_dimension=0, tiled=True)
    prompt_sum = lax.psum(prompt_part, "resp")
    resp_key_grad = resp_sum[:, :width].astype(jnp.bfloat16)
    resp_value_grad = resp_sum[:, width:].astype(jnp.bfloat16)
    prompt_key_grad = prompt_sum[:, :width].astype(jnp.bfloat16)
    prompt_value_grad = prompt_sum[:, width:].astype(jnp.bfloat16)
    return (
        attn_out[None],
        query_grad[None],
        resp_key_grad[None],
        resp_value_grad[None],
        prompt_key_grad,
        prompt_value_grad,
    )


def solution(mesh):
    in_specs = (
        P("resp", "ctx", None),
        P("resp", "ctx", None),
        P("resp", "ctx", None),
        P("ctx", None),
        P("ctx", None),
        P("resp", "ctx", None),
        P("resp"),
    )
    out_specs = (
        P("resp", "ctx", None),
        P("resp", "ctx", None),
        P("resp", "ctx", None),
        P("resp", "ctx", None),
        P("ctx", None),
        P("ctx", None),
    )
    return jax.shard_map(body, mesh=mesh, in_specs=in_specs, out_specs=out_specs, check_vma=False)
```

profile of v0, /device:TPU:8, one launch (start us, length us, event | category | flops | bytes accessed | tf_op | source)
XLA Modules:
  0.0 321.6 jit_solution(5401829585454170042)
XLA Ops:
  7.2 1.7 copy.163
  11.4 23.7 %all_gather.12 = bf16[512,512]{1,0:T(8,128)(2,1)S(1)} all-gather(bf16[32,512]{1,0:T(8,128)(2,1)} %param.14), channel_id=1, replica_groups=mesh['resp'=16,'ctx'=16] {'ctx'}, dimensions={0}, use_global_device_ids=true | all-gather | bytes 557056 | tf_op jit(solution)/shard_map/all_gather | solution.py:59
  35.3 20.1 %all_gather.14 = bf16[512,512]{1,0:T(8,128)(2,1)S(1)} all-gather(bf16[32,512]{1,0:T(8,128)(2,1)} %param.15), channel_id=1, replica_groups=mesh['resp'=16,'ctx'=16] {'ctx'}, dimensions={0}, use_global_device_ids=true | all-gather | bytes 557056 | tf_op jit(solution)/shard_map/all_gather | solution.py:60
  58.5 3.2 bitcast_reduce_fusion
  61.7 4.8 %fusion.39 = (f32[4,5,128]{2,1,0:T(8,128)S(1)}, f32[4,2048,128,5]{2,1,3,0:T(8,128)S(1)}) fusion(pred[128,2048]{0,1:T(8,128)(4,1)S(1)} %iota_compare_fusion, bf16[2048,4,128,1]{0,2,3,1:T(8,128)(2,1)} %bitcast.261, bf16[128,4,5,128]{0,3,2,1:T(8,128)(2,1)S(1)} %bitcast.245), kind=kOutput, calls=%fused_computation.49 | convolution fusion | flops 1357903360 | bytes 23996416 | tf_op jit(solution)/shard_map/nkgd,mkd->kgnm/dot_general | solution.py:15
  66.5 3.7 %fusion.43 = f32[4,5,128]{2,1,0:T(8,128)S(1)} fusion(f32[4,512,128,5]{2,1,3,0:T(8,128)} %get-tuple-element.374, f32[4,5,128]{2,1,0:T(8,128)S(1)} %get-tuple-element.371, pred[128]{0:T(512)(128)(4,1)S(1)} %broadcast_compare_fusion.2), kind=kLoop, calls=%fused_computation.56 | loop fusion | flops 5240320 | bytes 5263488 | tf_op jit(solution)/shard_map/reduce_sum | solution.py:51
  70.2 4.5 %exponential_reduce_fusion = f32[4,5,128]{2,1,0:T(8,128)S(1)} fusion(f32[4,2048,128,5]{2,1,3,0:T(8,128)S(1)} %get-tuple-element.376, f32[4,5,128]{2,1,0:T(8,128)S(1)} %get-tuple-element.372, pred[128,2048]{0,1:T(8,128)(4,1)S(1)} %iota_compare_fusion), kind=kLoop, calls=%fused_computation.48 | loop fusion | flops 20968960 | bytes 21254144 | tf_op jit(solution)/shard_map/reduce_sum | solution.py:51
  75.4 2.6 convolution_bitcast_fusion.1
  77.9 1.7 copy.169
  79.6 4.5 %reshape.290 = bf16[4,512,512]{1,0,2:T(4,128)(2,1)} reshape(bf16[1,2048,512]{1,2,0:T(8,128)(2,1)} %all-gather.5.cloned.1.call-done) | data formatting | bytes 4194304 | tf_op jit(solution)/shard_map/reshape | solution.py:25
  84.1 3.3 %copy.171 = bf16[4,512,512]{1,2,0:T(8,128)(2,1)} copy(bf16[4,512,512]{1,0,2:T(4,128)(2,1)} %reshape.290) | data formatting | bytes 4194304
  87.5 6.5 %all-gather.7.cloned.1.call-done = bf16[1,2048,512]{2,1,0:T(8,128)(2,1)} async-done(((bf16[1,128,512]{2,1,0:T(8,128)(2,1)}), bf16[1,2048,512]{2,1,0:T(8,128)(2,1)}) %all-gather.7.cloned.1.call-update) | async-done | bytes 2097168 | tf_op jit(solution)/shard_map/all_gather | solution.py:71
  93.9 4.1 %copy.170 = bf16[4,512,512]{1,2,0:T(8,128)(2,1)} copy(bf16[4,512,512]{2,1,0:T(8,128)(2,1)} %bitcast.267) | data formatting | bytes 4194304
  98.1 21.0 %while.6 = (s32[]{:T(128)}, f32[128,4,5,128]{0,3,2,1:T(8,128)S(1)}, bf16[4,512,512]{1,2,0:T(8,128)(2,1)}, s32[4,512]{1,0:T(4,128)S(1)}, bf16[4,512,512]{1,2,0:T(...) while((s32[]{:T(128)}, ...), condition=%wide.region_5.6_spmd.clone, body=%wide.region_4.5_spmd.clone.sunk | while | flops 676724864 | bytes 6571113 | solution.py:29
  100.1 3.1 fusion.108
  105.3 3.1 fusion.108
  110.6 3.1 fusion.108
  115.8 3.1 fusion.108
  119.2 1.9 fusion.48
  121.1 5.3 %fusion.50 = f32[4,128,512,1]{2,1,3,0:T(8,128)} fusion(bf16[128,4,5,128]{0,3,2,1:T(8,128)(2,1)S(1)} %get-tuple-element.536, f32[4,512,128,5]{2,1,3,0:T(8,128)} %get-tuple-element.374, f32[4,5,128]{2,1,0:T(8,128)} %get-tuple-element.581, pred[128]{0:T(512)(128)(4,1)S(1)} %broadcast_compare_fusion.3), kind=kOutput, calls=%fused_computation.75 | convolution fusion | flops 340787200 | bytes 6957184 | tf_op jit(solution)/shard_map/while/body/eval_jaxpr/kgnm,nkgd->mkd/dot_general | solution.py:125
  126.4 1.6 fusion.41
  130.1 2.5 copy.186
  133.9 3.1 pad_maximum_fusion
  137.1 1.5 copy.179
  138.6 69.7 %while.7 = (s32[]{:T(128)}, f32[128,4,5,128]{0,3,2,1:T(8,128)}, f32[4,512,1024]{2,1,0:T(8,128)}, bf16[4,512,512]{1,2,0:T(8,128)(2,1)}, s32[4,512]{1,0:T(4,128)S(...) while((s32[]{:T(128)}, f32[128,4,5,128]{0,3,2,1:T(8,128)}, ...), condition=%wide.region_7.8_spmd.clone, body=%wide.region_6.7_spmd.clone.sunk | while | flops 1692336256 | bytes 52139704 | solution.py:29
  141.0 1.7 fusion.120
  143.7 1.4 fusion.122
  145.1 1.5 maximum_bitcast_fusion.2
  146.7 2.9 copy.245
  149.6 3.2 constant_dynamic-update-slice_fusion.2
  152.8 3.2 fusion.121
  158.4 1.7 fusion.120
  162.5 1.5 maximum_bitcast_fusion.2
  164.1 2.9 copy.245
  167.0 3.2 constant_dynamic-update-slice_fusion.2
  170.2 3.2 fusion.121
  175.8 1.7 fusion.120
  179.9 1.5 maximum_bitcast_fusion.2
  181.5 2.9 copy.245
  184.4 3.2 constant_dynamic-update-slice_fusion.2
  187.6 3.2 fusion.121
  193.2 1.7 fusion.120
  197.4 1.5 maximum_bitcast_fusion.2
  198.9 2.9 copy.245
  201.8 3.2 constant_dynamic-update-slice_fusion.2
  205.0 3.2 fusion.121
  211.9 81.9 %all-reduce.1 = bf16[32,1024]{1,0:T(8,128)(2,1)S(1)} all-reduce(f32[32,1024]{1,0:T(8,128)} %reduce-scatter.5.cloned.1.call-done), channel_id=1, replica_groups=mesh['resp'=16,'ctx'=16] {'resp'}, use_global_device_ids=true, to_apply=%region_10.11 | all-reduce | flops 32768 | bytes 196608 | tf_op jit(solution)/shard_map/psum | solution.py:146
  294.5 18.8 %reduce-scatter.3.cloned.1.call-done = f32[128,1024]{1,0:T(8,128)} async-done(((f32[2048,1024]{1,0:T(8,128)}), f32[128,1024]{1,0:T(8,128)}) %reduce-scatter.3.cloned.1.call-update) | async-done | bytes 524304 | tf_op jit(solution)/shard_map/reduce_scatter | solution.py:141
  (127 shorter events, 41.1 us)
Async XLA Ops:
  7.2 50.2 %copy-start.4 = (bf16[1,128,2560]{2,1,0:T(8,128)(2,1)S(1)}, bf16[1,128,2560]{2,1,0:T(8,128)(2,1)}, u32[]{:S(2)}) copy-start(bf16[1,128,2560]{2,1,0:T(8,128)(2,1)} %param.16) | copy-start | bytes 1966084
  7.2 54.5 %all-gather.5.cloned.1.call-start = ((), (), s32[]{:S(2)}) async-start(), calls=%async_computation.4 | async-start | bytes 2228224 | tf_op jit(solution)/shard_map/all_gather | solution.py:70
  9.0 85.0 %all-gather.7.cloned.1.call-start = ((), (), s32[]{:S(2)}) async-start(), calls=%async_computation.5 | async-start | bytes 2228224 | tf_op jit(solution)/shard_map/all_gather | solution.py:71
  9.7 202.2 %reduce-scatter.5.cloned.1.call-start = ((), (), s32[]{:S(2)}) async-start(), calls=%async_computation.3 | async-start | bytes 2228224 | tf_op jit(solution)/shard_map/reduce_scatter | solution.py:145
  55.6 19.1 %copy-start.7 = (bf16[512,512]{0,1:T(8,128)(2,1)}, bf16[512,512]{0,1:T(8,128)(2,1)S(1)}, u32[]{:S(2)}) copy-start(bf16[512,512]{0,1:T(8,128)(2,1)S(1)} %copy.166) | copy-start | bytes 1572868
  66.5 8.9 %slice-start = ((s8[5242880]{0:T(1024)(128)(4,1)}), s8[4194304]{0:T(1024)(128)(4,1)S(1)}, s32[]{:S(2)}) async-start(s8[5242880]{0:T(1024)(128)(4,1)} %bitcast.252), calls=%async_computation.6 | async-start | bytes 8388608
  70.2 5.2 %slice-start.1 = ((s8[5242880]{0:T(1024)(128)(4,1)}), s8[1048576]{0:T(1024)(128)(4,1)S(1)}, s32[]{:S(2)}) async-start(s8[5242880]{0:T(1024)(128)(4,1)} %bitcast.252), calls=%async_computation.7 | async-start | bytes 2097152
  74.8 0.6 copy-start.11
  119.1 7.2 %copy-start.2 = (f32[128,4,5,128]{0,3,2,1:T(8,128)}, f32[128,4,5,128]{0,3,2,1:T(8,128)S(1)}, u32[]{:S(2)}) copy-start(f32[128,4,5,128]{0,3,2,1:T(8,128)S(1)} %get-tuple-element.157) | copy-start | bytes 3932164
  119.1 7.2 %slice-start.2 = ((s8[5242880]{0:T(1024)(128)(4,1)}), s8[4194304]{0:T(1024)(128)(4,1)S(1)}, s32[]{:S(2)}) async-start(s8[5242880]{0:T(1024)(128)(4,1)} %bitcast.254), calls=%async_computation.8 | async-start | bytes 8388608
  119.1 7.2 %copy-start.8 = (bf16[512,512]{0,1:T(8,128)(2,1)S(1)}, bf16[512,512]{0,1:T(8,128)(2,1)}, u32[]{:S(2)}) copy-start(bf16[512,512]{0,1:T(8,128)(2,1)} %copy-done.7) | copy-start | bytes 1572868
  119.1 7.2 %copy-start.12 = (f32[4,5,128]{2,1,0:T(8,128)S(1)}, f32[4,5,128]{2,1,0:T(8,128)}, u32[]{:S(2)}) copy-start(f32[4,5,128]{2,1,0:T(8,128)} %get-tuple-element.581) | copy-start | bytes 30724
  121.0 7.0 %copy-start.5 = (bf16[128,4,5,128]{0,3,2,1:T(8,128)(2,1)}, bf16[128,4,5,128]{0,3,2,1:T(8,128)(2,1)S(1)}, u32[]{:S(2)}) copy-start(bf16[128,4,5,128]{0,3,2,1:T(8,128)(2,1)S(1)} %get-tuple-element.536) | copy-start | bytes 1966084
  121.0 7.0 %copy-start.9 = (f32[4,5,128]{2,1,0:T(8,128)}, f32[4,5,128]{2,1,0:T(8,128)S(1)}, u32[]{:S(2)}) copy-start(f32[4,5,128]{2,1,0:T(8,128)S(1)} %get-tuple-element.537) | copy-start | bytes 30724
  121.1 5.3 %slice-start.3 = ((s8[5242880]{0:T(1024)(128)(4,1)}), s8[1048576]{0:T(1024)(128)(4,1)S(1)}, s32[]{:S(2)}) async-start(s8[5242880]{0:T(1024)(128)(4,1)} %bitcast.254), calls=%async_computation.9 | async-start | bytes 2097152
  132.6 5.9 %copy-start.10 = (f32[4,5,128]{2,1,0:T(8,128)S(1)}, f32[4,5,128]{2,1,0:T(8,128)}, u32[]{:S(2)}) copy-start(f32[4,5,128]{2,1,0:T(8,128)} %copy-done.9) | copy-start | bytes 30724
  132.6 5.9 %copy-start.13 = (f32[4,5,128]{2,1,0:T(8,128)S(1)}, f32[4,5,128]{2,1,0:T(8,128)}, u32[]{:S(2)}) copy-start(f32[4,5,128]{2,1,0:T(8,128)} %get-tuple-element.581) | copy-start | bytes 30724
  137.0 176.3 %reduce-scatter.3.cloned.1.call-start = ((), (), s32[]{:S(2)}) async-start(), calls=%async_computation.2 | async-start | bytes 8912896 | tf_op jit(solution)/shard_map/reduce_scatter | solution.py:141
  138.6 2.4 copy-start.6
  139.9 1.1 copy-start
  156.0 2.4 copy-start.6
  157.3 1.1 copy-start
  173.4 2.4 copy-start.6
  174.7 1.1 copy-start
  190.8 2.4 copy-start.6
  192.1 1.1 copy-start
  208.2 1.3 copy-start.1
  208.2 2.5 copy-start.3
Sparse Core Ops, SparseCore 0:
  10.4 43.8 all-gather.4
  56.1 37.7 all-gather.6
  137.1 66.8 reduce-scatter.4
  208.4 104.8 reduce-scatter.2
where the time goes:
time: 323 us; the launch traced here: 322 us
  blocking collectives  126 us (39%)
  local copies, waits for them, and re-layouts  65.2 us (20%)
  matrix products  64.7 us (20%)
  waiting for transfers between devices  26 us (8%)
  other arithmetic  24.4 us (8%)
  between operations  14.7 us (5%)
    psum x1, blocking collectives, body(): prompt_sum = lax.psum(prompt_part, 'resp')  81.9 us
    dynamic_update_slice x8, local copies, waits for them, and re-layouts, scan_blocks(): return lax.scan(step, init, blocks)  24.5 us
    all_gather x1, blocking collectives, body(): lax.all_gather(prompt_keys, 'ctx', axis=0, tiled=True)  23.7 us
    all_gather x1, blocking collectives, body(): lax.all_gather(prompt_values, 'ctx', axis=0, tiled=True)  20.1 us
    unnamed x42, local copies, waits for them, and re-layouts  20 us
    reduce_scatter x1, waiting for transfers between devices, body(): lax.psum_scatter(resp_terms.reshape(seq_rows, 2 * width), 'ctx', scatter_...  18.8 us
    dot_general x5, matrix products, out_step(): jnp.einsum('kgnm,mkd->nkgd', prob, values3, preferred_element_type=jnp.fl...  15.1 us
    dot_general x5, matrix products, grads_block(): jnp.einsum('kgnm,mkd->nkgd', dscore, keys3, preferred_element_type=jnp.fl...  13.8 us
  transfers between devices with their start and end apart: 4, of which 2 were waited for; matrix products, arithmetic and copies ran while one was open for 33% of the time, Pallas kernels for 0%

commit v1 on v0

--- a/solution.py
+++ b/solution.py
@@ -68,7 +68,9 @@
     top, total, prompt_kbuf, prompt_vbuf = (top, total, key_buf, value_buf)
     pieces = (
         lax.all_gather(resp_keys[0], "ctx", axis=0, tiled=True),
-        lax.all_gather(resp_values[0], "ctx", axis=0, tiled=True),
+        jnp.concatenate(
+            lax.all_to_all(jnp.stack([resp_values[0]] * lax.axis_size("ctx")), "ctx", 0, 0), axis=0
+        ),
     )
     top, total, key_buf, value_buf = (
         top,

time: 323 us -> 347 us (1.074)
  blocking collectives: 126 us -> 152 us
  waiting for transfers between devices: 26 us -> 16.8 us
  starting transfers between devices: 0.16 us -> 6.06 us
    all_gather x1, blocking collectives: 23.7 us -> 46.6 us  [body(): lax.all_gather(prompt_keys, 'ctx', axis=0, tiled=True)]
    all_gather x1 -> x0, waiting for transfers between devices: 6.47 us -> none  [body(): lax.all_gather(resp_values[0], 'ctx', axis=0, tiled=True)]
    all_to_all x0 -> x1, starting transfers between devices: none -> 5.94 us  [body(): lax.all_to_all(jnp.stack([resp_values[0]] * lax.axis_size('ctx')), 'ctx',...]
    unnamed x42 -> x48, local copies, waits for them, and re-layouts: 20 us -> 19 us
  transfers between devices with their start and end apart: 4 -> 4, of which waited for: 2 -> 1; matrix products, arithmetic and copies ran while one was open for 33% -> 31% of each run, Pallas kernels for 0% -> 0%
where the time goes in v1:
time: 347 us; the launch traced here: 346 us
  blocking collectives  152 us (44%)
  local copies, waits for them, and re-layouts  66.5 us (19%)
  matrix products  65 us (19%)
  other arithmetic  24.3 us (7%)
  waiting for transfers between devices  16.8 us (5%)
  between operations  14.8 us (4%)
  starting transfers between devices  6.06 us (2%)
    psum x1, blocking collectives, body(): prompt_sum = lax.psum(prompt_part, 'resp')  84.3 us
    all_gather x1, blocking collectives, body(): lax.all_gather(prompt_keys, 'ctx', axis=0, tiled=True)  46.6 us
    dynamic_update_slice x8, local copies, waits for them, and re-layouts, scan_blocks(): return lax.scan(step, init, blocks)  24.4 us
    all_gather x1, blocking collectives, body(): lax.all_gather(prompt_values, 'ctx', axis=0, tiled=True)  21.3 us
    unnamed x48, local copies, waits for them, and re-layouts  19 us
    reduce_scatter x1, waiting for transfers between devices, body(): lax.psum_scatter(resp_terms.reshape(seq_rows, 2 * width), 'ctx', scatter_...  16.7 us
    dot_general x5, matrix products, out_step(): jnp.einsum('kgnm,mkd->nkgd', prob, values3, preferred_element_type=jnp.fl...  15.1 us
    dot_general x5, matrix products, grads_block(): jnp.einsum('kgnm,mkd->nkgd', dscore, keys3, preferred_element_type=jnp.fl...  14 us
  transfers between devices with their start and end apart: 4, of which 1 were waited for; matrix products, arithmetic and copies ran while one was open for 31% of the time, Pallas kernels for 0%

profile of v1, /device:TPU:8, one launch (start us, length us, event | category | flops | bytes accessed | tf_op | source)
XLA Modules:
  0.0 346.2 jit_solution(865267304290936259)
XLA Ops:
  7.2 1.7 copy.163
  9.0 2.4 stack.3
  11.4 5.9 %all-to-all-start = ((bf16[16,128,512]{2,1,0:T(8,128)(2,1)}), bf16[16,128,512]{2,1,0:T(8,128)(2,1)}, u32[]{:S(2)}, u32[]{:S(2)}) async-start(bf16[16,128,512]{2,1,0:T(8,128)(2,1)} %stack.3), calls=%async_computation | async-start | bytes 4194304 | tf_op jit(solution)/shard_map/all_to_all | solution.py:72
  17.8 46.6 %all_gather.9 = bf16[512,512]{1,0:T(8,128)(2,1)S(1)} all-gather(bf16[32,512]{1,0:T(8,128)(2,1)S(1)} %copy-done.10), channel_id=1, replica_groups=mesh['resp'=16,'ctx'=16] {'ctx'}, dimensions={0}, use_global_device_ids=true | all-gather | bytes 557056 | tf_op jit(solution)/shard_map/all_gather | solution.py:59
  64.6 21.3 %all_gather.11 = bf16[512,512]{1,0:T(8,128)(2,1)S(1)} all-gather(bf16[32,512]{1,0:T(8,128)(2,1)S(1)} %copy-done.11), channel_id=1, replica_groups=mesh['resp'=16,'ctx'=16] {'ctx'}, dimensions={0}, use_global_device_ids=true | all-gather | bytes 557056 | tf_op jit(solution)/shard_map/all_gather | solution.py:60
  89.2 3.3 bitcast_reduce_fusion
  92.5 4.8 %fusion.39 = (f32[4,5,128]{2,1,0:T(8,128)S(1)}, f32[4,2048,128,5]{2,1,3,0:T(8,128)S(1)}) fusion(pred[128,2048]{0,1:T(8,128)(4,1)S(1)} %iota_compare_fusion, bf16[2048,4,128,1]{0,2,3,1:T(8,128)(2,1)} %bitcast.262, bf16[128,4,5,128]{0,3,2,1:T(8,128)(2,1)S(1)} %bitcast.246), kind=kOutput, calls=%fused_computation.49 | convolution fusion | flops 1357903360 | bytes 23996416 | tf_op jit(solution)/shard_map/nkgd,mkd->kgnm/dot_general | solution.py:15
  97.4 3.7 %fusion.43 = f32[4,5,128]{2,1,0:T(8,128)S(1)} fusion(f32[4,512,128,5]{2,1,3,0:T(8,128)} %get-tuple-element.374, f32[4,5,128]{2,1,0:T(8,128)S(1)} %get-tuple-element.371, pred[128]{0:T(512)(128)(4,1)S(1)} %broadcast_compare_fusion.2), kind=kLoop, calls=%fused_computation.56 | loop fusion | flops 5240320 | bytes 5263488 | tf_op jit(solution)/shard_map/reduce_sum | solution.py:51
  101.0 4.5 %exponential_reduce_fusion = f32[4,5,128]{2,1,0:T(8,128)S(1)} fusion(f32[4,2048,128,5]{2,1,3,0:T(8,128)S(1)} %get-tuple-element.376, f32[4,5,128]{2,1,0:T(8,128)S(1)} %get-tuple-element.372, pred[128,2048]{0,1:T(8,128)(4,1)S(1)} %iota_compare_fusion), kind=kLoop, calls=%fused_computation.48 | loop fusion | flops 20968960 | bytes 21254144 | tf_op jit(solution)/shard_map/reduce_sum | solution.py:51
  106.2 2.6 convolution_bitcast_fusion.1
  108.8 1.7 copy.169
  110.5 4.5 %reshape.286 = bf16[4,512,512]{1,0,2:T(4,128)(2,1)} reshape(bf16[1,2048,512]{1,2,0:T(8,128)(2,1)} %all-gather.3.cloned.1.call-done) | data formatting | bytes 4194304 | tf_op jit(solution)/shard_map/reshape | solution.py:25
  115.0 3.3 copy.171
  118.3 4.1 %copy.170 = bf16[4,512,512]{1,2,0:T(8,128)(2,1)} copy(bf16[4,512,512]{2,1,0:T(8,128)(2,1)} %bitcast.15) | data formatting | bytes 4194304
  122.4 21.0 %while.6 = (s32[]{:T(128)}, f32[128,4,5,128]{0,3,2,1:T(8,128)S(1)}, bf16[4,512,512]{1,2,0:T(8,128)(2,1)}, s32[4,512]{1,0:T(4,128)S(1)}, bf16[4,512,512]{1,2,0:T(...) while((s32[]{:T(128)}, ...), condition=%wide.region_5.6_spmd.clone, body=%wide.region_4.5_spmd.clone.sunk | while | flops 676724864 | bytes 6571113 | solution.py:29
  124.5 3.1 fusion.108
  129.7 3.1 fusion.108
  134.9 3.1 fusion.108
  140.2 3.1 fusion.108
  143.5 1.9 fusion.48
  145.4 5.2 %fusion.50 = f32[4,128,512,1]{2,1,3,0:T(8,128)} fusion(bf16[128,4,5,128]{0,3,2,1:T(8,128)(2,1)S(1)} %get-tuple-element.536, f32[4,512,128,5]{2,1,3,0:T(8,128)} %get-tuple-element.374, f32[4,5,128]{2,1,0:T(8,128)} %get-tuple-element.577, pred[128]{0:T(512)(128)(4,1)S(1)} %broadcast_compare_fusion.3), kind=kOutput, calls=%fused_computation.75 | convolution fusion | flops 340787200 | bytes 6957184 | tf_op jit(solution)/shard_map/while/body/eval_jaxpr/kgnm,nkgd->mkd/dot_general | solution.py:127
  150.7 1.6 fusion.41
  154.4 2.6 copy.186
  158.2 3.2 pad_maximum_fusion
  161.5 1.5 copy.179
  163.0 69.5 %while.7 = (s32[]{:T(128)}, f32[128,4,5,128]{0,3,2,1:T(8,128)}, f32[4,512,1024]{2,1,0:T(8,128)}, bf16[4,512,512]{1,2,0:T(8,128)(2,1)}, s32[4,512]{1,0:T(4,128)S(...) while((s32[]{:T(128)}, f32[128,4,5,128]{0,3,2,1:T(8,128)}, ...), condition=%wide.region_7.8_spmd.clone, body=%wide.region_6.7_spmd.clone.sunk | while | flops 1692336256 | bytes 52139704 | solution.py:29
  165.4 1.7 fusion.120
  169.6 1.5 maximum_bitcast_fusion.2
  171.0 2.9 copy.245
  173.9 3.2 constant_dynamic-update-slice_fusion.2
  177.1 3.2 fusion.121
  182.8 1.7 fusion.120
  186.9 1.5 maximum_bitcast_fusion.2
  188.4 2.9 copy.245
  191.3 3.2 constant_dynamic-update-slice_fusion.2
  194.5 3.2 fusion.121
  200.1 1.7 fusion.120
  204.3 1.5 maximum_bitcast_fusion.2
  205.7 2.9 copy.245
  208.7 3.2 constant_dynamic-update-slice_fusion.2
  211.9 3.2 fusion.121
  217.5 1.7 fusion.120
  221.7 1.5 maximum_bitcast_fusion.2
  223.1 2.9 copy.245
  226.1 3.2 constant_dynamic-update-slice_fusion.2
  229.3 3.2 fusion.121
  236.2 84.3 %all-reduce.1 = bf16[32,1024]{1,0:T(8,128)(2,1)S(1)} all-reduce(f32[32,1024]{1,0:T(8,128)} %reduce-scatter.5.cloned.1.call-done), channel_id=1, replica_groups=mesh['resp'=16,'ctx'=16] {'resp'}, use_global_device_ids=true, to_apply=%region_10.11 | all-reduce | flops 32768 | bytes 196608 | tf_op jit(solution)/shard_map/psum | solution.py:148
  321.1 16.7 %reduce-scatter.3.cloned.1.call-done = f32[128,1024]{1,0:T(8,128)} async-done(((f32[2048,1024]{1,0:T(8,128)}), f32[128,1024]{1,0:T(8,128)}) %reduce-scatter.3.cloned.1.call-update) | async-done | bytes 524304 | tf_op jit(solution)/shard_map/reduce_scatter | solution.py:143
  (133 shorter events, 40.7 us)
Async XLA Ops:
  7.2 10.3 %copy-start.4 = (bf16[1,128,2560]{2,1,0:T(8,128)(2,1)S(1)}, bf16[1,128,2560]{2,1,0:T(8,128)(2,1)}, u32[]{:S(2)}) copy-start(bf16[1,128,2560]{2,1,0:T(8,128)(2,1)} %param.11) | copy-start | bytes 1966084
  7.2 10.6 %copy-start.10 = (bf16[32,512]{1,0:T(8,128)(2,1)S(1)}, bf16[32,512]{1,0:T(8,128)(2,1)}, u32[]{:S(2)}) copy-start(bf16[32,512]{1,0:T(8,128)(2,1)} %param.14) | copy-start | bytes 98308
  7.2 57.4 %copy-start.11 = (bf16[32,512]{1,0:T(8,128)(2,1)S(1)}, bf16[32,512]{1,0:T(8,128)(2,1)}, u32[]{:S(2)}) copy-start(bf16[32,512]{1,0:T(8,128)(2,1)} %param.15) | copy-start | bytes 98308
  7.2 85.3 %all-gather.3.cloned.1.call-start = ((), (), s32[]{:S(2)}) async-start(), calls=%async_computation.5 | async-start | bytes 2228224 | tf_op jit(solution)/shard_map/all_gather | solution.py:70
  11.4 76.5 %copy-start.5 = (bf16[1,128,2560]{2,1,0:T(8,128)(2,1)S(1)}, bf16[1,128,2560]{2,1,0:T(8,128)(2,1)}, u32[]{:S(2)}) copy-start(bf16[1,128,2560]{2,1,0:T(8,128)(2,1)} %param.16) | copy-start | bytes 1966084
  11.4 106.9 %all-to-all-start = ((bf16[16,128,512]{2,1,0:T(8,128)(2,1)}), bf16[16,128,512]{2,1,0:T(8,128)(2,1)}, u32[]{:S(2)}, u32[]{:S(2)}) async-start(bf16[16,128,512]{2,1,0:T(8,128)(2,1)} %stack.3), calls=%async_computation | async-start | bytes 4194304 | tf_op jit(solution)/shard_map/all_to_all | solution.py:72
  17.4 218.9 %reduce-scatter.5.cloned.1.call-start = ((), (), s32[]{:S(2)}) async-start(), calls=%async_computation.4 | async-start | bytes 2228224 | tf_op jit(solution)/shard_map/reduce_scatter | solution.py:147
  86.1 19.5 %copy-start.8 = (bf16[512,512]{0,1:T(8,128)(2,1)}, bf16[512,512]{0,1:T(8,128)(2,1)S(1)}, u32[]{:S(2)}) copy-start(bf16[512,512]{0,1:T(8,128)(2,1)S(1)} %copy.166) | copy-start | bytes 1572868
  97.3 8.9 %slice-start = ((s8[5242880]{0:T(1024)(128)(4,1)}), s8[4194304]{0:T(1024)(128)(4,1)S(1)}, s32[]{:S(2)}) async-start(s8[5242880]{0:T(1024)(128)(4,1)} %bitcast.253), calls=%async_computation.6 | async-start | bytes 8388608
  101.0 5.2 %slice-start.1 = ((s8[5242880]{0:T(1024)(128)(4,1)}), s8[1048576]{0:T(1024)(128)(4,1)S(1)}, s32[]{:S(2)}) async-start(s8[5242880]{0:T(1024)(128)(4,1)} %bitcast.253), calls=%async_computation.7 | async-start | bytes 2097152
  105.6 0.6 copy-start.14
  143.5 7.2 %copy-start.2 = (f32[128,4,5,128]{0,3,2,1:T(8,128)}, f32[128,4,5,128]{0,3,2,1:T(8,128)S(1)}, u32[]{:S(2)}) copy-start(f32[128,4,5,128]{0,3,2,1:T(8,128)S(1)} %get-tuple-element.157) | copy-start | bytes 3932164
  143.5 7.2 %slice-start.2 = ((s8[5242880]{0:T(1024)(128)(4,1)}), s8[4194304]{0:T(1024)(128)(4,1)S(1)}, s32[]{:S(2)}) async-start(s8[5242880]{0:T(1024)(128)(4,1)} %bitcast.255), calls=%async_computation.8 | async-start | bytes 8388608
  143.5 7.1 %copy-start.9 = (bf16[512,512]{0,1:T(8,128)(2,1)S(1)}, bf16[512,512]{0,1:T(8,128)(2,1)}, u32[]{:S(2)}) copy-start(bf16[512,512]{0,1:T(8,128)(2,1)} %copy-done.8) | copy-start | bytes 1572868
  143.5 7.1 %copy-start.15 = (f32[4,5,128]{2,1,0:T(8,128)S(1)}, f32[4,5,128]{2,1,0:T(8,128)}, u32[]{:S(2)}) copy-start(f32[4,5,128]{2,1,0:T(8,128)} %get-tuple-element.577) | copy-start | bytes 30724
  145.4 6.9 %copy-start.6 = (bf16[128,4,5,128]{0,3,2,1:T(8,128)(2,1)}, bf16[128,4,5,128]{0,3,2,1:T(8,128)(2,1)S(1)}, u32[]{:S(2)}) copy-start(bf16[128,4,5,128]{0,3,2,1:T(8,128)(2,1)S(1)} %get-tuple-element.536) | copy-start | bytes 1966084
  145.4 6.9 %copy-start.12 = (f32[4,5,128]{2,1,0:T(8,128)}, f32[4,5,128]{2,1,0:T(8,128)S(1)}, u32[]{:S(2)}) copy-start(f32[4,5,128]{2,1,0:T(8,128)S(1)} %get-tuple-element.537) | copy-start | bytes 30724
  145.4 5.2 %slice-start.3 = ((s8[5242880]{0:T(1024)(128)(4,1)}), s8[1048576]{0:T(1024)(128)(4,1)S(1)}, s32[]{:S(2)}) async-start(s8[5242880]{0:T(1024)(128)(4,1)} %bitcast.255), calls=%async_computation.9 | async-start | bytes 2097152
  156.9 6.0 %copy-start.13 = (f32[4,5,128]{2,1,0:T(8,128)S(1)}, f32[4,5,128]{2,1,0:T(8,128)}, u32[]{:S(2)}) copy-start(f32[4,5,128]{2,1,0:T(8,128)} %copy-done.12) | copy-start | bytes 30724
  156.9 6.0 %copy-start.16 = (f32[4,5,128]{2,1,0:T(8,128)S(1)}, f32[4,5,128]{2,1,0:T(8,128)}, u32[]{:S(2)}) copy-start(f32[4,5,128]{2,1,0:T(8,128)} %get-tuple-element.577) | copy-start | bytes 30724
  161.4 176.4 %reduce-scatter.3.cloned.1.call-start = ((), (), s32[]{:S(2)}) async-start(), calls=%async_computation.3 | async-start | bytes 8912896 | tf_op jit(solution)/shard_map/reduce_scatter | solution.py:143
  163.0 2.4 copy-start.7
  164.3 1.1 copy-start
  180.3 2.4 copy-start.7
  181.7 1.1 copy-start
  197.7 2.4 copy-start.7
  199.0 1.1 copy-start
  215.1 2.4 copy-start.7
  216.4 1.1 copy-start
  232.5 1.3 copy-start.1
  232.5 2.5 copy-start.3
Sparse Core Ops, SparseCore 0:
  10.4 55.6 all-gather.2
  161.5 67.2 reduce-scatter.4
  232.7 105.1 reduce-scatter.2
